TPU v7x, 32 devices: a whole 2x2x4 slice. The times are simulated.
32 devices in a mesh: level: 8 (over z, x), slab: 4 (over y, core).
Axes of the slice: x: 2, y: 2, z: 4, core: 2. Of those that a mesh axis runs over, the one named last changes fastest.
Arguments:
- trajectory: float32 [8, 8, 8, 32, 128], P('level', None, 'slab'), may hold values from -6 to 6
- first_latent: float32 [8, 8, 32, 128], P(None, 'slab'), may hold values from -6 to 6
- noise_draw: float32 [8, 8, 8, 32, 128], P('level', None, 'slab'), may hold values from -6 to 6
- w_in: bfloat16 [64, 8, 3, 3, 3], replicated, may hold values from -0.4375 to 0.4375
- bias_in: float32 [64], replicated, may hold values from -3 to 3
- level_bias: float32 [8, 64], P('level'), may hold values from -3 to 3
- w_out: bfloat16 [8, 64, 3, 3, 3], replicated, may hold values from -0.15625 to 0.15625
- bias_out: float32 [8], replicated, may hold values from -2 to 2
- drift_coef: float32 [8], P('level'), may hold values from -0.12 to -0.02
- eps_coef: float32 [8], P('level'), may hold values from 0.05 to 0.3
- noise_coef: float32 [8], P('level'), may hold values from 0.05 to 0.2
Outputs:
- next_states: float32 [8, 8, 8, 32, 128], P('level', None, 'slab')
All inputs are finite; a program needn't handle non-finite values.
Results may differ from a plain program's by a relative error of at most 0.0016.
Values may be sent and summed in bfloat16 or wider, within the bound.
A program may use at most 64 MiB of HBM per device.

v0:
```python
import jax
import jax.numpy as jnp
from jax import lax
from jax.sharding import PartitionSpec as P

ITERS = 2


def with_halo(cells, sides, width):
    for axis, dim in sides:
        count = lax.axis_size(axis)
        ends = count - 1
        head = lax.slice_in_dim(cells, 0, width, axis=dim)
        tail = lax.slice_in_dim(cells, cells.shape[dim] - width, cells.shape[dim], axis=dim)
        cells = jnp.concatenate(
            [
                lax.ppermute(tail, axis, [(i, (i + 1) % count) for i in range(ends)]),
                cells,
                lax.ppermute(head, axis, [((i + 1) % count, i) for i in range(ends)]),
            ],
            axis=dim,
        )
    return cells


def entering(shard, axis, combine, identity):
    count, index = (lax.axis_size(axis), lax.axis_index(axis))
    everything = lax.all_gather(shard, axis)
    start = jnp.broadcast_to(jnp.asarray(identity, shard.dtype), shard.shape)

    def step(k, before):
        reached = k < index
        new = combine(before, everything[k])
        return jnp.where(reached, new, before)

    return lax.fori_loop(0, count, step, start)


def convolve(field, kernel, depth_pad):
    return lax.conv_general_dilated(
        field[None],
        kernel,
        (1, 1, 1),
        ((depth_pad, depth_pad), (1, 1), (1, 1)),
        dimension_numbers=("NCDHW", "OIDHW", "NCDHW"),
        preferred_element_type=jnp.float32,
    )[0]


def add_terms(earlier, later):
    return earlier + later


def on_device(
    trajectory,
    first_latent,
    noise_draw,
    w_in,
    bias_in,
    level_bias,
    w_out,
    bias_out,
    drift_coef,
    eps_coef,
    noise_coef,
):
    current = trajectory[0]
    fresh = noise_draw[0]
    shift_in = (bias_in + level_bias[0])[:, None, None, None]
    depth = current.shape[1]
    slab_index = lax.axis_index("slab")
    slab_count = lax.axis_size("slab")
    result = current
    for step in range(ITERS):
        latent_bf = current.astype(jnp.bfloat16)
        padded = with_halo(latent_bf, (("slab", 1),), 2)
        before = convolve(padded, w_in, 0)
        planes = slab_index * depth - 1 + jnp.arange(depth + 2, dtype=jnp.int32)
        inside = (planes >= 0) & (planes < slab_count * depth)
        activated = jax.nn.silu(before + shift_in)
        hidden_padded = jnp.where(inside[None, :, None, None], activated, 0.0).astype(jnp.bfloat16)
        predicted = convolve(hidden_padded, w_out, 0) + bias_out[:, None, None, None]
        increment = drift_coef[0] * current + eps_coef[0] * predicted + noise_coef[0] * fresh
        earlier = entering(increment, "level", add_terms, jnp.zeros_like(increment))
        if step + 1 < ITERS:
            current = first_latent + earlier
        else:
            result = first_latent + (earlier + increment)
    return result[None]


def solution(mesh):
    placed = (
        P("level", None, "slab", None, None),
        P(None, "slab", None, None),
        P("level", None, "slab", None, None),
        P(),
        P(),
        P("level", None),
        P(),
        P(),
        P("level"),
        P("level"),
        P("level"),
    )
    return jax.shard_map(
        on_device,
        mesh=mesh,
        in_specs=placed,
        out_specs=P("level", None, "slab", None, None),
        check_vma=False,
    )
```

profile of v0, /device:TPU:24, one launch (start us, length us, event | category | flops | bytes accessed | tf_op | source)
XLA Modules:
  0.0 239.4 jit_solution(18280087790933491827)
XLA Ops:
  7.5 1.7 collective-permute-start
  9.3 1.3 collective-permute-start.1
  15.1 5.2 %copy.78 = bf16[8,6,32,1,8,17]{0,4,5,2,1,3:T(8,128)(2,1)} copy(bf16[8,6,32,1,8,17]{2,0,5,4,1,3:T(8,128)(2,1)S(1)} %bitcast.72) | data formatting | bytes 835584 | tf_op jit(solution)/shard_map/conv_general_dilated | solution.py:40
  20.3 1.4 slice.8
  21.7 14.1 %select_bitcast_fusion.1 = bf16[4,32,1,8,17,64]{5,3,4,1,0,2:T(8,128)(2,1)S(1)} fusion(f32[64]{0:T(128)S(1)} %bitcast_add_fusion.2, pred[4]{0:T(512)(128)(4,1)S(1)} %compare_and_fusion, pred[8,17]{0,1:T(8,128)(4,1)S(1)} %copy-done.6, bf16[64,8,3,3,3]{0,1,4,3,2:T(8,128)(2,1)S(1)} %copy-done, bf16[8,6,32,1,7,2]{0,4,5,2,1,3:T(8,128)(2,1)S(1)} %slice.8, ...), kind=kOutput, calls=%fused_computation.44 | convolution fusion | flops 482697216 | bytes 2717068 | tf_op jit(solution)/shard_map/conv_general_dilated | solution.py:40
  36.0 18.4 %fusion.23 = f32[2,32,8,17,8]{4,2,3,1,0:T(8,128)} fusion(bf16[8,64,3,3,3]{1,0,4,3,2:T(8,128)(2,1)S(1)} %copy-done.5, bf16[4,32,1,7,1,64]{5,3,4,1,0,2:T(8,128)(2,1)S(1)} %get-tuple-element.230, bf16[4,32,1,7,1,64]{5,3,4,1,0,2:T(8,128)(2,1)S(1)} %get-tuple-element.229, bf16[4,32,1,8,17,64]{5,3,4,1,0,2:T(8,128)(2,1)S(1)} %select_bitcast_fusion.1), kind=kOutput, calls=%fused_computation.28 | convolution fusion | flops 248086528 | bytes 2763776 | tf_op jit(solution)/shard_map/conv_general_dilated | solution.py:40
  54.4 3.0 %copy.79 = f32[2,32,8,17,8]{1,4,3,2,0:T(8,128)S(1)} copy(f32[2,32,8,17,8]{4,2,3,1,0:T(8,128)} %fusion.23) | data formatting | bytes 557056 | tf_op jit(solution)/shard_map/conv_general_dilated | solution.py:40
  58.9 51.1 %all-gather.4.cloned.1.call-done = f32[8,8,2,32,128]{4,3,2,1,0:T(8,128)} async-done(((f32[1,8,2,32,128]{4,3,2,1,0:T(8,128)}), f32[8,8,2,32,128]{4,3,2,1,0:T(8,128)}) %all-gather.4.cloned.1.call-update) | async-done | bytes 2097168 | tf_op jit(solution)/shard_map/all_gather | solution.py:28
  110.0 8.6 %while.28 = (s32[]{:T(128)}, f32[8,2,32,128]{3,2,1,0:T(8,128)S(1)}, s32[]{:T(128)}, f32[8,8,2,32,128]{4,3,2,1,0:T(8,128)}, s32[]{:T(128)}, /*index=5*/s32[]{:T(128)}) while((s32[]{:T(128)}, f32[8,2,32,128]{3,2,1,0:T(8,128)S(1)}, s32[]{:T(128)}, f32[8,8,2,32,128]{4,3,2,1,0:T(8,128)}, s32[]{:T(128)}, /*index=5*/s32[]{:T(128)}) %tuple.65), condition=%wide.region_1.2_spmd.clone, body=%wide.region_0.1_spmd.clone.sunk | while | flops 196612 | bytes 786525 | solution.py:36
  111.0 1.1 add_select_fusion.4
  112.1 1.1 add_select_fusion.4
  113.2 1.1 add_select_fusion.4
  114.3 1.1 add_select_fusion.4
  115.3 1.1 add_select_fusion.4
  116.4 1.1 add_select_fusion.4
  117.5 1.1 add_select_fusion.4
  118.6 1.7 collective-permute-start.2
  120.3 1.3 collective-permute-start.3
  121.6 3.2 %collective-permute-done.3 = bf16[8,2,32,128]{3,2,1,0:T(8,128)(2,1)S(1)} collective-permute-done((bf16[8,2,32,128]{3,2,1,0:T(8,128)(2,1)S(1)}, bf16[8,2,32,128]{3,2,1,0:T(8,128)(2,1)S(1)}, u32[]{:S(2)}, u32[]{:S(2)}) %collective-permute-start.3) | collective-permute-done | bytes 131104 | tf_op jit(solution)/shard_map/ppermute | solution.py:19
  124.9 1.9 copy.88
  126.8 1.7 pad.4.clone
  128.6 5.2 %copy.83 = bf16[8,6,32,1,8,17]{0,4,5,2,1,3:T(8,128)(2,1)} copy(bf16[8,6,32,1,8,17]{2,0,5,4,1,3:T(8,128)(2,1)S(1)} %bitcast.71) | data formatting | bytes 835584 | tf_op jit(solution)/shard_map/conv_general_dilated | solution.py:40
  133.8 1.4 slice.12
  135.1 14.1 %select_bitcast_fusion = bf16[4,32,1,8,17,64]{5,3,4,1,0,2:T(8,128)(2,1)S(1)} fusion(f32[64]{0:T(128)S(1)} %bitcast_add_fusion.2, pred[4]{0:T(512)(128)(4,1)S(1)} %compare_and_fusion, pred[8,17]{0,1:T(8,128)(4,1)S(1)} %copy-done.6, bf16[64,8,3,3,3]{0,1,4,3,2:T(8,128)(2,1)S(1)} %copy-done, bf16[8,6,32,1,7,2]{0,4,5,2,1,3:T(8,128)(2,1)S(1)} %slice.12, ...), kind=kOutput, calls=%fused_computation.43 | convolution fusion | flops 482697216 | bytes 2717068 | tf_op jit(solution)/shard_map/conv_general_dilated | solution.py:40
  149.4 18.5 %fusion.28 = f32[2,32,8,17,8]{4,2,3,1,0:T(8,128)} fusion(bf16[8,64,3,3,3]{1,0,4,3,2:T(8,128)(2,1)S(1)} %copy-done.5, bf16[4,32,1,7,1,64]{5,3,4,1,0,2:T(8,128)(2,1)S(1)} %get-tuple-element.228, bf16[4,32,1,7,1,64]{5,3,4,1,0,2:T(8,128)(2,1)S(1)} %get-tuple-element.227, bf16[4,32,1,8,17,64]{5,3,4,1,0,2:T(8,128)(2,1)S(1)} %select_bitcast_fusion), kind=kOutput, calls=%fused_computation.32 | convolution fusion | flops 248086528 | bytes 2763776 | tf_op jit(solution)/shard_map/conv_general_dilated | solution.py:40
  167.9 2.9 %copy.84 = f32[2,32,8,17,8]{1,4,3,2,0:T(8,128)S(1)} copy(f32[2,32,8,17,8]{4,2,3,1,0:T(8,128)} %fusion.28) | data formatting | bytes 557056 | tf_op jit(solution)/shard_map/conv_general_dilated | solution.py:40
  172.1 50.2 %all-gather.6.cloned.1.call-done = f32[64,2,32,128]{3,2,1,0:T(8,128)} async-done(((f32[8,2,32,128]{3,2,1,0:T(8,128)}), f32[64,2,32,128]{3,2,1,0:T(8,128)}) %all-gather.6.cloned.1.call-update) | async-done | bytes 2097168 | tf_op jit(solution)/shard_map/all_gather | solution.py:28
  222.3 8.6 %while.29 = (s32[]{:T(128)}, f32[8,2,32,128]{3,2,1,0:T(8,128)S(1)}, s32[]{:T(128)}, f32[8,8,2,32,128]{4,3,2,1,0:T(8,128)}, s32[]{:T(128)}, /*index=5*/s32[]{:T(128)}) while((s32[]{:T(128)}, f32[8,2,32,128]{3,2,1,0:T(8,128)S(1)}, s32[]{:T(128)}, f32[8,8,2,32,128]{4,3,2,1,0:T(8,128)}, s32[]{:T(128)}, /*index=5*/s32[]{:T(128)}) %tuple.75), condition=%wide.region_3.4_spmd.clone, body=%wide.region_2.3_spmd.clone.sunk | while | flops 196612 | bytes 786525 | solution.py:36
  223.4 1.1 add_select_fusion.5
  226.6 1.1 add_select_fusion.5
  227.7 1.1 add_select_fusion.5
  230.9 1.7 add_bitcast_fusion
  (46 shorter events, 12.8 us)
Async XLA Ops:
  6.5 15.2 %copy-start = (bf16[64,8,3,3,3]{0,1,4,3,2:T(8,128)(2,1)S(1)}, bf16[64,8,3,3,3]{0,1,4,3,2:T(8,128)(2,1)}, u32[]{:S(2)}) copy-start(bf16[64,8,3,3,3]{0,1,4,3,2:T(8,128)(2,1)} %param.18) | copy-start | bytes 82948
  6.5 103.4 %all-gather.4.cloned.1.call-start = ((), (), s32[]{:S(2)}) async-start(), calls=%async_computation | async-start | bytes 2359296 | tf_op jit(solution)/shard_map/all_gather | solution.py:28
  7.5 5.7 %collective-permute-start = (bf16[8,2,32,128]{3,2,1,0:T(8,128)(2,1)S(1)}, bf16[8,2,32,128]{3,2,1,0:T(8,128)(2,1)S(1)}, u32[]{:S(2)}, u32[]{:S(2)}) collective-permute-start(bf16[8,2,32,128]{3,2,1,0:T(8,128)(2,1)S(1)} %convert_bitcast_fusion), channel_id=1, source_target_pairs={{0,1},{1,2},{2,3},{4,5},{5,6},{6,7},{8,9},{9,10},{10,11},{12,13},{... | collective-permute-start | bytes 393224 | tf_op jit(solution)/shard_map/ppermute | solution.py:17
  9.3 4.5 %collective-permute-start.1 = (bf16[8,2,32,128]{3,2,1,0:T(8,128)(2,1)S(1)}, bf16[8,2,32,128]{3,2,1,0:T(8,128)(2,1)S(1)}, u32[]{:S(2)}, u32[]{:S(2)}) collective-permute-start(bf16[8,2,32,128]{3,2,1,0:T(8,128)(2,1)S(1)} %convert_bitcast_fusion), channel_id=1, source_target_pairs={{1,0},{2,1},{3,2},{5,4},{6,5},{7,6},{9,8},{10,9},{11,10},{13,12},{... | collective-permute-start | bytes 393224 | tf_op jit(solution)/shard_map/ppermute | solution.py:19
  14.8 6.9 %copy-start.6 = (pred[8,17]{0,1:T(8,128)(4,1)S(1)}, pred[8,17]{0,1:T(8,128)(4,1)}, u32[]{:S(2)}) copy-start(pred[8,17]{0,1:T(8,128)(4,1)} %constant.91) | copy-start | bytes 412
  21.7 14.3 %copy-start.5 = (bf16[8,64,3,3,3]{1,0,4,3,2:T(8,128)(2,1)S(1)}, bf16[8,64,3,3,3]{1,0,4,3,2:T(8,128)(2,1)}, u32[]{:S(2)}) copy-start(bf16[8,64,3,3,3]{1,0,4,3,2:T(8,128)(2,1)} %param.21) | copy-start | bytes 82948
  36.0 21.4 %copy-start.4 = (f32[8]{0:T(128)S(1)}, f32[8]{0:T(128)}, u32[]{:S(2)}) copy-start(f32[8]{0:T(128)} %param.22) | copy-start | bytes 100
  54.4 3.6 %copy-start.2 = (f32[1,8,2,32,128]{4,3,2,1,0:T(8,128)S(1)}, f32[1,8,2,32,128]{4,3,2,1,0:T(8,128)}, u32[]{:S(2)}) copy-start(f32[1,8,2,32,128]{4,3,2,1,0:T(8,128)} %param.17) | copy-start | bytes 786436
  54.4 3.6 %copy-start.3 = (f32[1,8,2,32,128]{4,3,2,1,0:T(8,128)S(1)}, f32[1,8,2,32,128]{4,3,2,1,0:T(8,128)}, u32[]{:S(2)}) copy-start(f32[1,8,2,32,128]{4,3,2,1,0:T(8,128)} %param.15) | copy-start | bytes 786436
  57.4 61.2 %copy-start.1 = (f32[8,2,32,128]{3,2,1,0:T(8,128)S(1)}, f32[8,2,32,128]{3,2,1,0:T(8,128)}, u32[]{:S(2)}) copy-start(f32[8,2,32,128]{3,2,1,0:T(8,128)} %param.16) | copy-start | bytes 786436
  58.8 163.5 %all-gather.6.cloned.1.call-start = ((), (), s32[]{:S(2)}) async-start(), calls=%async_computation.1 | async-start | bytes 2359296 | tf_op jit(solution)/shard_map/all_gather | solution.py:28
  118.6 3.0 %collective-permute-start.2 = (bf16[8,2,32,128]{3,2,1,0:T(8,128)(2,1)S(1)}, bf16[8,2,32,128]{3,2,1,0:T(8,128)(2,1)S(1)}, u32[]{:S(2)}, u32[]{:S(2)}) collective-permute-start(bf16[8,2,32,128]{3,2,1,0:T(8,128)(2,1)S(1)} %add_convert_fusion), channel_id=1, source_target_pairs={{0,1},{1,2},{2,3},{4,5},{5,6},{6,7},{8,9},{9,10},{10,11},{12,13},{... | collective-permute-start | bytes 393224 | tf_op jit(solution)/shard_map/ppermute | solution.py:17
  120.3 4.6 %collective-permute-start.3 = (bf16[8,2,32,128]{3,2,1,0:T(8,128)(2,1)S(1)}, bf16[8,2,32,128]{3,2,1,0:T(8,128)(2,1)S(1)}, u32[]{:S(2)}, u32[]{:S(2)}) collective-permute-start(bf16[8,2,32,128]{3,2,1,0:T(8,128)(2,1)S(1)} %add_convert_fusion), channel_id=1, source_target_pairs={{1,0},{2,1},{3,2},{5,4},{6,5},{7,6},{9,8},{10,9},{11,10},{13,12},{... | collective-permute-start | bytes 393224 | tf_op jit(solution)/shard_map/ppermute | solution.py:19
Sparse Core Ops, SparseCore 0:
  58.9 50.9 all-gather.3
  172.2 50.0 all-gather.5
where the time goes:
time: 244 us; the launch traced here: 239 us
  waiting for transfers between devices  105 us (43%)
  matrix products  65.1 us (27%)
  local copies, waits for them, and re-layouts  25.1 us (10%)
  other arithmetic  22.1 us (9%)
  between operations  15.6 us (6%)
  starting transfers between devices  6.06 us (2%)
    all_gather x2, waiting for transfers between devices, entering(): everything = lax.all_gather(shard, axis)  101 us
    conv_general_dilated x4, matrix products, convolve(): lax.conv_general_dilated(field[None], kernel, (1, 1, 1), ((depth_pad, dep...  65.1 us
    conv_general_dilated x7, local copies, waits for them, and re-layouts, convolve(): lax.conv_general_dilated(field[None], kernel, (1, 1, 1), ((depth_pad, dep...  19.1 us
    select_n x16, other arithmetic, step(): return jnp.where(reached, new, before)  16.8 us
  transfers between devices with their start and end apart: 6, of which 4 were waited for; matrix products, arithmetic and copies ran while one was open for 0% of the time, Pallas kernels for 0%

commit v1 on v0

v1 whole, which is shorter than its diff:
```python
import functools

import jax
import jax.numpy as jnp
from jax import lax
from jax.experimental import pallas as pl
from jax.experimental.pallas import tpu as pltpu
from jax.sharding import PartitionSpec as P

ITERS = 2
MESH = pl.DeviceIdType.MESH
F32 = jnp.float32
BF16 = jnp.bfloat16


def kernel(
    dims,
    traj, first, noise, w_in, bias_in, level_bias, w_out, bias_out, drift, eps, nco,
    out,
    a1, a2, bias_col, cur, base, xs, y, inc, sb, hl, hr, xsb, xr, zsb, zr, xr_last, zsb_last, zr_last,
    hs_sem, hr_sem, x_ssem, x_rsem, z_ssem, z_rsem,
):
    chans, hid, depth, rows, width, levels, slabs, chunk, block = dims
    level, slab = lax.axis_index("level"), lax.axis_index("slab")
    odd = lax.rem(level, 2)
    group = lax.div(level, 2)
    groups = levels // 2
    partner = level + 1 - 2 * odd
    stride = depth * rows
    own = depth * chans
    side = 2 * chans
    full = depth + 4
    mid = depth + 2
    chunks = rows // chunk
    lanes = lax.broadcasted_iota(jnp.int32, (1, width), 1)
    not_first = lanes > 0
    not_last = lanes < width - 1

    barrier = pltpu.get_barrier_semaphore()
    pl.semaphore_signal(barrier, inc=1, device_id={"level": partner}, device_id_type=MESH)

    @pl.when(group > 0)
    def _():
        pl.semaphore_signal(barrier, inc=1, device_id={"level": level - 2}, device_id_type=MESH)

    @pl.when(group < groups - 1)
    def _():
        pl.semaphore_signal(barrier, inc=1, device_id={"level": level + 2}, device_id_type=MESH)

    @pl.when(slab > 0)
    def _():
        pl.semaphore_signal(barrier, inc=1, device_id={"slab": slab - 1}, device_id_type=MESH)

    @pl.when(slab < slabs - 1)
    def _():
        pl.semaphore_signal(barrier, inc=1, device_id={"slab": slab + 1}, device_id_type=MESH)

    def one(cond):
        return jnp.where(cond, 1, 0)

    def rows_of(ref, h):
        return jnp.concatenate(
            [ref[pl.ds(d * rows + h, chans, stride=stride), :] for d in range(depth)], axis=0
        )

    def at(h, n=1, pad=0):
        return pl.ds(pl.multiple_of((h + pad) * width, width), n * width)

    @pl.loop(0, chunks)
    def _(j):
        for r in range(chunk):
            h = j * chunk + r
            v = rows_of(traj, h)
            cur[:, at(h)] = v
            sb[0, :, at(h)] = v.astype(BF16)

    pl.semaphore_wait(
        barrier,
        1 + one(group > 0) + one(group < groups - 1) + one(slab > 0) + one(slab < slabs - 1),
    )

    def halo_copies(it, j, span):
        to_right = pltpu.make_async_remote_copy(
            src_ref=sb.at[it, pl.ds(own - side, side), span],
            dst_ref=hl.at[it, :, span],
            send_sem=hs_sem.at[it, 0, j],
            recv_sem=hr_sem.at[it, 0, j],
            device_id={"slab": slab + 1},
            device_id_type=MESH,
        )
        to_left = pltpu.make_async_remote_copy(
            src_ref=sb.at[it, pl.ds(0, side), span],
            dst_ref=hr.at[it, :, span],
            send_sem=hs_sem.at[it, 1, j],
            recv_sem=hr_sem.at[it, 1, j],
            device_id={"slab": slab - 1},
            device_id_type=MESH,
        )
        return to_right, to_left

    def halo_start(it, j):
        to_right, to_left = halo_copies(it, j, at(j * chunk, chunk))

        @pl.when(slab < slabs - 1)
        def _():
            to_right.start()

        @pl.when(slab > 0)
        def _():
            to_left.start()

    def halo_recv(it, j):
        to_right, to_left = halo_copies(it, j, at(j * chunk, chunk))

        @pl.when(slab > 0)
        def _():
            to_right.wait_recv()

        @pl.when(slab < slabs - 1)
        def _():
            to_left.wait_recv()

    def halo_sent(it, j):
        to_right, to_left = halo_copies(it, j, at(j * chunk, chunk))

        @pl.when(slab < slabs - 1)
        def _():
            to_right.wait_send()

        @pl.when(slab > 0)
        def _():
            to_left.wait_send()

    def wires(it):
        if it == ITERS - 1:
            return inc, xr_last, zsb_last, zr_last
        return xsb.at[it], xr.at[it], zsb.at[it], zr.at[it]

    def pair_copy(it, j):
        span = at(j * chunk, chunk)
        src, dst, _, _ = wires(it)
        return pltpu.make_async_remote_copy(
            src_ref=src.at[:, span],
            dst_ref=dst.at[:, span],
            send_sem=x_ssem.at[it, j],
            recv_sem=x_rsem.at[it, j],
            device_id={"level": partner},
            device_id_type=MESH,
        )

    def chain_copy(it, j):
        span = at(j * chunk, chunk)
        _, _, src, dst = wires(it)
        return pltpu.make_async_remote_copy(
            src_ref=src.at[:, span],
            dst_ref=dst.at[:, span],
            send_sem=z_ssem.at[it, j],
            recv_sem=z_rsem.at[it, j],
            device_id={"level": level + 2},
            device_id_type=MESH,
        )

    @pl.loop(0, chunks)
    def _(j):
        halo_start(0, j)

    @pl.when(slab == 0)
    def _():
        hl[...] = jnp.zeros_like(hl)

    @pl.when(slab == slabs - 1)
    def _():
        hr[...] = jnp.zeros_like(hr)

    @pl.when(group == 0)
    def _():
        zr[...] = jnp.zeros_like(zr)
        zr_last[...] = jnp.zeros_like(zr_last)

    for ref, dtype in ((xs, BF16), (y, F32)):
        n = ref.shape[0]
        ref[:, 0:width] = jnp.zeros((n, width), dtype)
        ref[:, (rows + 1) * width:(rows + 2) * width] = jnp.zeros((n, width), dtype)

    def tap(ref, n, kd, kh, kw):
        row = ((kd * 3 + kh) * 3 + kw) * n
        return ref[row:row + n, :]

    w_in, w_out = w_in[...].astype(F32), w_out[...].astype(F32)
    zero = jnp.zeros((chans, hid), F32)
    parts = []
    for kh in range(3):
        for kw in range(3):
            for q in range(full):
                parts.append(jnp.concatenate(
                    [tap(w_in, chans, q - p, kh, kw) if 0 <= q - p < 3 else zero for p in range(mid)],
                    axis=1,
                ))
    a1[...] = (0.5 * jnp.concatenate(parts, axis=0)).T.astype(BF16)

    keep = [jnp.float32(1.0)] * mid
    keep[0] = jnp.where(slab > 0, 1.0, 0.0).astype(F32)
    keep[-1] = jnp.where(slab < slabs - 1, 1.0, 0.0).astype(F32)
    parts = []
    for kh in range(3):
        for kw in range(3):
            for d in range(depth):
                parts.append(jnp.concatenate(
                    [tap(w_out, chans, p - d, kh, kw) * keep[p] if 0 <= p - d < 3 else zero for p in range(mid)],
                    axis=1,
                ))
    a2[...] = jnp.concatenate(parts, axis=0).astype(BF16)

    shift = jnp.broadcast_to(0.5 * (bias_in[...] + level_bias[...]), (width, hid)).T
    bias_col[...] = jnp.concatenate([shift] * mid, axis=0)
    tail = jnp.broadcast_to(bias_out[...] * eps[0], (width, chans)).T
    tail = jnp.concatenate([tail] * depth, axis=0)

    @pl.loop(0, chunks)
    def _(j):
        for r in range(chunk):
            h = j * chunk + r
            base[:, at(h)] = rows_of(noise, h) * nco[0] + tail

    drift_v, eps_v = drift[0], eps[0]

    for it in range(ITERS):
        last = it == ITERS - 1
        _, pair_in, chain_out, chain_in = wires(it)

        @pl.loop(0, chunks)
        def _(j):
            halo_recv(it, j)
            for r in range(chunk):
                h = j * chunk + r
                v = jnp.concatenate(
                    [hl[it, :, at(h)], sb[it, :, at(h)], hr[it, :, at(h)]], axis=0
                ).astype(F32)
                n = full * chans
                xs[0:n, at(h, pad=1)] = jnp.where(not_first, pltpu.roll(v, 1, 1), 0.0).astype(BF16)
                xs[n:2 * n, at(h, pad=1)] = v.astype(BF16)
                xs[2 * n:3 * n, at(h, pad=1)] = jnp.where(
                    not_last, pltpu.roll(v, width - 1, 1), 0.0).astype(BF16)

        @pl.loop(0, rows // block)
        def _(b):
            h = b * block
            field = jnp.concatenate([xs[:, at(h, block, kh)] for kh in range(3)], axis=0)
            u = jnp.dot(a1[...], field, preferred_element_type=F32)
            u = u + jnp.concatenate([bias_col[...]] * block, axis=1)
            hidden = (u + u * jnp.tanh(u)).astype(BF16)
            y[:, at(h, block, 1)] = jnp.dot(a2[...], hidden, preferred_element_type=F32)

        @pl.loop(0, chunks)
        def _(j):
            for r in range(chunk):
                h = j * chunk + r
                taps = []
                for kw in range(3):
                    acc = None
                    for kh in range(3):
                        row = (kh * 3 + kw) * own
                        v = y[row:row + own, at(h, pad=kh)]
                        acc = v if acc is None else acc + v
                    taps.append(acc)
                pred = taps[1] + jnp.where(not_first, pltpu.roll(taps[0], 1, 1), 0.0)
                pred = pred + jnp.where(not_last, pltpu.roll(taps[2], width - 1, 1), 0.0)
                v = drift_v * cur[:, at(h)] + (eps_v * pred + base[:, at(h)])
                inc[:, at(h)] = v
                if not last:
                    xsb[it, :, at(h)] = v.astype(BF16)
            pair_copy(it, j).start()

        @pl.loop(0, chunks)
        def _(j):
            pair_copy(it, j).wait_recv()

            @pl.when(group > 0)
            def _():
                chain_copy(it, j).wait_recv()

            span = at(j * chunk, chunk)

            @pl.when(group < groups - 1)
            def _():
                total = chain_in[:, span].astype(F32) + (inc[:, span] + pair_in[:, span].astype(F32))
                chain_out[:, span] = total.astype(chain_out.dtype)
                chain_copy(it, j).start()

            odd_f = odd.astype(F32)
            for r in range(chunk):
                h = j * chunk + r
                v = rows_of(first, h) + (chain_in[:, at(h)].astype(F32) + odd_f * pair_in[:, at(h)].astype(F32))
                if last:
                    v = v + inc[:, at(h)]
                    for d in range(depth):
                        out[pl.ds(d * rows + h, chans, stride=stride), :] = v[d * chans:(d + 1) * chans]
                else:
                    cur[:, at(h)] = v
                    sb[it + 1, :, at(h)] = v.astype(BF16)
            if not last:
                halo_start(it + 1, j)

    @pl.loop(0, chunks)
    def _(j):
        for it in range(ITERS):
            halo_sent(it, j)
            pair_copy(it, j).wait_send()

            @pl.when(group < groups - 1)
            def _():
                chain_copy(it, j).wait_send()


def on_device(levels, slabs, trajectory, first_latent, noise_draw, w_in, bias_in, level_bias,
              w_out, bias_out, drift_coef, eps_coef, noise_coef):
    _, chans, depth, rows, width = trajectory.shape
    hid = w_in.shape[0]
    chunk = 8 if rows % 8 == 0 else rows
    block = 4 if rows % 4 == 0 else rows
    chunks = rows // chunk
    own, side = depth * chans, 2 * chans
    full, mid = depth + 4, depth + 2
    area = rows * width
    padded = (rows + 2) * width
    flat = chans * depth * rows
    dims = (chans, hid, depth, rows, width, levels, slabs, chunk, block)
    vmem = pl.BlockSpec(memory_space=pltpu.VMEM)
    smem = pl.BlockSpec(memory_space=pltpu.SMEM)
    dma = pltpu.SemaphoreType.DMA
    result = pl.pallas_call(
        functools.partial(kernel, dims),
        out_shape=jax.ShapeDtypeStruct((flat, width), F32),
        in_specs=[vmem] * 8 + [smem] * 3,
        out_specs=vmem,
        scratch_shapes=[
            pltpu.VMEM((mid * hid, 9 * full * chans), BF16),
            pltpu.VMEM((9 * own, mid * hid), BF16),
            pltpu.VMEM((mid * hid, width), F32),
            pltpu.VMEM((own, area), F32),
            pltpu.VMEM((own, area), F32),
            pltpu.VMEM((3 * full * chans, padded), BF16),
            pltpu.VMEM((9 * own, padded), F32),
            pltpu.VMEM((own, area), F32),
            pltpu.VMEM((ITERS, own, area), BF16),
            pltpu.VMEM((ITERS, side, area), BF16),
            pltpu.VMEM((ITERS, side, area), BF16),
            pltpu.VMEM((ITERS - 1, own, area), BF16),
            pltpu.VMEM((ITERS - 1, own, area), BF16),
            pltpu.VMEM((ITERS - 1, own, area), BF16),
            pltpu.VMEM((ITERS - 1, own, area), BF16),
            pltpu.VMEM((own, area), F32),
            pltpu.VMEM((own, area), F32),
            pltpu.VMEM((own, area), F32),
            dma((ITERS, 2, chunks)),
            dma((ITERS, 2, chunks)),
            dma((ITERS, chunks)),
            dma((ITERS, chunks)),
            dma((ITERS, chunks)),
            dma((ITERS, chunks)),
        ],
        compiler_params=pltpu.CompilerParams(
            collective_id=0, has_side_effects=True, vmem_limit_bytes=48 * 1024 * 1024
        ),
    )(
        trajectory.reshape(flat, width),
        first_latent.reshape(flat, width),
        noise_draw.reshape(flat, width),
        jnp.transpose(w_in, (2, 3, 4, 1, 0)).reshape(27 * chans, hid),
        bias_in[None],
        level_bias,
        jnp.transpose(w_out, (2, 3, 4, 0, 1)).reshape(27 * chans, hid),
        bias_out[None],
        drift_coef,
        eps_coef,
        noise_coef,
    )
    return result.reshape(trajectory.shape)


def solution(mesh):
    placed = (
        P("level", None, "slab", None, None),
        P(None, "slab", None, None),
        P("level", None, "slab", None, None),
        P(),
        P(),
        P("level", None),
        P(),
        P(),
        P("level"),
        P("level"),
        P("level"),
    )
    return jax.shard_map(
        functools.partial(on_device, mesh.shape["level"], mesh.shape["slab"]),
        mesh=mesh,
        in_specs=placed,
        out_specs=P("level", None, "slab", None, None),
        check_vma=False,
    )
```

time: 244 us -> 43.5 us (0.18); the launches traced: 239 us -> 43.1 us
  waiting for transfers between devices: 105 us -> 0 us
  matrix products: 65.1 us -> 0 us
  Pallas kernels: 0 us -> 35.3 us
  other arithmetic: 22.1 us -> 0 us
  local copies, waits for them, and re-layouts: 25.1 us -> 5.84 us
  between operations: 15.6 us -> 1.98 us
  starting transfers between devices: 6.06 us -> 0 us
    all_gather x2 -> x0, waiting for transfers between devices: 101 us -> none  [entering(): everything = lax.all_gather(shard, axis)]
    conv_general_dilated x4 -> x0, matrix products: 65.1 us -> none  [convolve(): lax.conv_general_dilated(field[None], kernel, (1, 1, 1), ((depth_pad, dep...]
    pallas_call x0 -> x1, Pallas kernels: none -> 35.3 us  [on_device(): pl.pallas_call(functools.partial(kernel, dims), out_shape=jax.ShapeDtypeS...]
    conv_general_dilated x7 -> x0, local copies, waits for them, and re-layouts: 19.1 us -> none  [convolve(): lax.conv_general_dilated(field[None], kernel, (1, 1, 1), ((depth_pad, dep...]
    select_n x16 -> x0, other arithmetic: 16.8 us -> none  [step(): return jnp.where(reached, new, before)]
    ppermute x4 -> x0, starting transfers between devices: 6.01 us -> none  [the longest x2 3.43 us: with_halo(): lax.ppermute(tail, axis, [(i, (i + 1) % count) for i in range(ends)])]
    ppermute x4 -> x0, waiting for transfers between devices: 3.85 us -> none  [the longest x2 3.84 us: with_halo(): lax.ppermute(head, axis, [((i + 1) % count, i) for i in range(ends)])]
    unnamed x17, local copies, waits for them, and re-layouts: 2.7 us -> 5.84 us
  transfers between devices with their start and end apart: 6 -> 0, of which waited for: 4 -> 0; matrix products, arithmetic and copies ran while one was open for 0% -> 0% of each run, Pallas kernels for 0% -> 0%
where the time goes in v1:
time: 43.5 us; the launch traced here: 43.1 us
  Pallas kernels  35.3 us (81%)
  local copies, waits for them, and re-layouts  5.84 us (13%)
  between operations  1.98 us (5%)
    pallas_call x1, Pallas kernels, on_device(): pl.pallas_call(functools.partial(kernel, dims), out_shape=jax.ShapeDtypeS...  35.3 us
    unnamed x17, local copies, waits for them, and re-layouts  5.84 us

profile of v1, /device:TPU:24, one launch (start us, length us, event | category | flops | bytes accessed | tf_op | source)
XLA Modules:
  0.0 43.1 jit_solution(11711532564175273101)
XLA Ops:
  1.9 0.0 copy-start.5
  2.0 0.0 copy-start.6
  2.0 0.0 copy-start.7
  2.0 0.6 %copy-done.5 = f32[64]{0:T(128)S(1)} copy-done((f32[64]{0:T(128)S(1)}, f32[64]{0:T(128)}, u32[]{:S(2)}) %copy-start.5) | copy-done | bytes 280
  2.6 0.0 copy-done.6
  2.6 0.0 copy-done.7
  2.6 0.0 copy-start
  2.6 0.9 %copy-done = f32[1,8,2,32,128]{4,3,2,1,0:T(8,128)S(1)} copy-done((f32[1,8,2,32,128]{4,3,2,1,0:T(8,128)S(1)}, f32[1,8,2,32,128]{4,3,2,1,0:T(8,128)}, u32[]{:S(2)}) %copy-start) | copy-done | bytes 262168
  3.6 0.0 copy-start.1
  3.6 0.9 %copy-done.1 = f32[8,2,32,128]{3,2,1,0:T(8,128)S(1)} copy-done((f32[8,2,32,128]{3,2,1,0:T(8,128)S(1)}, f32[8,2,32,128]{3,2,1,0:T(8,128)}, u32[]{:S(2)}) %copy-start.1) | copy-done | bytes 262168
  4.5 0.0 copy-start.2
  4.5 0.9 %copy-done.2 = f32[1,8,2,32,128]{4,3,2,1,0:T(8,128)S(1)} copy-done((f32[1,8,2,32,128]{4,3,2,1,0:T(8,128)S(1)}, f32[1,8,2,32,128]{4,3,2,1,0:T(8,128)}, u32[]{:S(2)}) %copy-start.2) | copy-done | bytes 262168
  5.5 0.0 copy-start.3
  5.5 0.8 %copy-done.3 = bf16[64,8,3,3,3]{0,1,4,3,2:T(8,128)(2,1)S(1)} copy-done((bf16[64,8,3,3,3]{0,1,4,3,2:T(8,128)(2,1)S(1)}, bf16[64,8,3,3,3]{0,1,4,3,2:T(8,128)(2,1)}, u32[]{:S(2)}) %copy-start.3) | copy-done | bytes 27672
  6.3 0.0 copy-start.4
  6.3 0.8 %copy-done.4 = bf16[8,64,3,3,3]{1,0,4,3,2:T(8,128)(2,1)S(1)} copy-done((bf16[8,64,3,3,3]{1,0,4,3,2:T(8,128)(2,1)S(1)}, bf16[8,64,3,3,3]{1,0,4,3,2:T(8,128)(2,1)}, u32[]{:S(2)}) %copy-start.4) | copy-done | bytes 27672
  7.1 35.3 %shard_map.109 = f32[512,128]{1,0:T(8,128)S(1)} custom-call(f32[512,128]{1,0:T(8,128)S(1)} %bitcast.13, f32[512,128]{1,0:T(8,128)S(1)} %bitcast.14, f32[512,128]{1,0:T(8,128)S(1)} %bitcast.15, bf16[216,64]{1,0:T(8,128)(2,1)S(1)} %bitcast.16, f32[1,64]{1,0:T(1,128)S(1)} %bitcast.18, f32[1,64]{1,0:T(1,128)S(1)} %copy-done.6, bf16[216,64]{1,0:T(8,128)(2,1)S(1)} %bitcast.17, ...), custom_call_target="tpu_custom_call" | custom-call | tf_op jit(solution)/shard_map/pallas_call | solution.py:331
  42.4 0.7 %copy.16 = f32[1,8,2,32,128]{4,3,2,1,0:T(8,128)} copy(f32[1,8,2,32,128]{4,3,2,1,0:T(8,128)S(1)} %bitcast.12) | data formatting | bytes 524288
Async XLA Ops:
  1.9 0.7 %copy-start.5 = (f32[64]{0:T(128)S(1)}, f32[64]{0:T(128)}, u32[]{:S(2)}) copy-start(f32[64]{0:T(128)} %param.15) | copy-start | bytes 772
  2.0 0.7 %copy-start.6 = (f32[1,64]{1,0:T(1,128)S(1)}, f32[1,64]{1,0:T(1,128)}, u32[]{:S(2)}) copy-start(f32[1,64]{1,0:T(1,128)} %level_bias.1) | copy-start | bytes 772
  2.0 0.7 %copy-start.7 = (f32[8]{0:T(128)S(1)}, f32[8]{0:T(128)}, u32[]{:S(2)}) copy-start(f32[8]{0:T(128)} %param.18) | copy-start | bytes 100
  2.6 0.9 %copy-start = (f32[1,8,2,32,128]{4,3,2,1,0:T(8,128)S(1)}, f32[1,8,2,32,128]{4,3,2,1,0:T(8,128)}, u32[]{:S(2)}) copy-start(f32[1,8,2,32,128]{4,3,2,1,0:T(8,128)} %param.11) | copy-start | bytes 786436
  3.6 0.9 %copy-start.1 = (f32[8,2,32,128]{3,2,1,0:T(8,128)S(1)}, f32[8,2,32,128]{3,2,1,0:T(8,128)}, u32[]{:S(2)}) copy-start(f32[8,2,32,128]{3,2,1,0:T(8,128)} %param.12) | copy-start | bytes 786436
  4.5 0.9 %copy-start.2 = (f32[1,8,2,32,128]{4,3,2,1,0:T(8,128)S(1)}, f32[1,8,2,32,128]{4,3,2,1,0:T(8,128)}, u32[]{:S(2)}) copy-start(f32[1,8,2,32,128]{4,3,2,1,0:T(8,128)} %param.13) | copy-start | bytes 786436
  5.5 0.8 %copy-start.3 = (bf16[64,8,3,3,3]{0,1,4,3,2:T(8,128)(2,1)S(1)}, bf16[64,8,3,3,3]{0,1,4,3,2:T(8,128)(2,1)}, u32[]{:S(2)}) copy-start(bf16[64,8,3,3,3]{0,1,4,3,2:T(8,128)(2,1)} %param.14) | copy-start | bytes 82948
  6.3 0.8 %copy-start.4 = (bf16[8,64,3,3,3]{1,0,4,3,2:T(8,128)(2,1)S(1)}, bf16[8,64,3,3,3]{1,0,4,3,2:T(8,128)(2,1)}, u32[]{:S(2)}) copy-start(bf16[8,64,3,3,3]{1,0,4,3,2:T(8,128)(2,1)} %param.17) | copy-start | bytes 82948

commit v2 on v1

--- a/solution.py
+++ b/solution.py
@@ -8,6 +8,7 @@
 from jax.sharding import PartitionSpec as P
 
 ITERS = 2
+LAG = 5
 MESH = pl.DeviceIdType.MESH
 F32 = jnp.float32
 BF16 = jnp.bfloat16
@@ -15,8 +16,10 @@
 
 def kernel(
     dims,
-    traj, first, noise, w_in, bias_in, level_bias, w_out, bias_out, drift, eps, nco,
+    traj_hbm, first_hbm, noise_hbm, w_in_hbm, w_out_hbm,
+    bias_in, level_bias, bias_out, drift, eps, nco,
     out,
+    traj, first, noise, w_in, w_out, in_sem,
     a1, a2, bias_col, cur, base, xs, y, inc, sb, hl, hr, xsb, xr, zsb, zr, xr_last, zsb_last, zr_last,
     hs_sem, hr_sem, x_ssem, x_rsem, z_ssem, z_rsem,
 ):
@@ -36,6 +39,15 @@
     not_first = lanes > 0
     not_last = lanes < width - 1
 
+    fetches = [
+        pltpu.make_async_copy(src, dst, in_sem.at[i])
+        for i, (src, dst) in enumerate((
+            (traj_hbm, traj), (w_in_hbm, w_in), (w_out_hbm, w_out), (noise_hbm, noise), (first_hbm, first),
+        ))
+    ]
+    for fetch in fetches:
+        fetch.start()
+
     barrier = pltpu.get_barrier_semaphore()
     pl.semaphore_signal(barrier, inc=1, device_id={"level": partner}, device_id_type=MESH)
 
@@ -65,6 +77,8 @@
 
     def at(h, n=1, pad=0):
         return pl.ds(pl.multiple_of((h + pad) * width, width), n * width)
+
+    fetches[0].wait()
 
     @pl.loop(0, chunks)
     def _(j):
@@ -186,6 +200,8 @@
         row = ((kd * 3 + kh) * 3 + kw) * n
         return ref[row:row + n, :]
 
+    fetches[1].wait()
+    fetches[2].wait()
     w_in, w_out = w_in[...].astype(F32), w_out[...].astype(F32)
     zero = jnp.zeros((chans, hid), F32)
     parts = []
@@ -216,20 +232,22 @@
     tail = jnp.broadcast_to(bias_out[...] * eps[0], (width, chans)).T
     tail = jnp.concatenate([tail] * depth, axis=0)
 
+    fetches[3].wait()
+
     @pl.loop(0, chunks)
     def _(j):
         for r in range(chunk):
             h = j * chunk + r
             base[:, at(h)] = rows_of(noise, h) * nco[0] + tail
 
+    fetches[4].wait()
     drift_v, eps_v = drift[0], eps[0]
 
     for it in range(ITERS):
         last = it == ITERS - 1
         _, pair_in, chain_out, chain_in = wires(it)
 
-        @pl.loop(0, chunks)
-        def _(j):
+        def build(j):
             halo_recv(it, j)
             for r in range(chunk):
                 h = j * chunk + r
@@ -242,8 +260,7 @@
                 xs[2 * n:3 * n, at(h, pad=1)] = jnp.where(
                     not_last, pltpu.roll(v, width - 1, 1), 0.0).astype(BF16)
 
-        @pl.loop(0, rows // block)
-        def _(b):
+        def convolve(b):
             h = b * block
             field = jnp.concatenate([xs[:, at(h, block, kh)] for kh in range(3)], axis=0)
             u = jnp.dot(a1[...], field, preferred_element_type=F32)
@@ -251,8 +268,7 @@
             hidden = (u + u * jnp.tanh(u)).astype(BF16)
             y[:, at(h, block, 1)] = jnp.dot(a2[...], hidden, preferred_element_type=F32)
 
-        @pl.loop(0, chunks)
-        def _(j):
+        def combine(j):
             for r in range(chunk):
                 h = j * chunk + r
                 taps = []
@@ -271,8 +287,7 @@
                     xsb[it, :, at(h)] = v.astype(BF16)
             pair_copy(it, j).start()
 
-        @pl.loop(0, chunks)
-        def _(j):
+        def scan(j):
             pair_copy(it, j).wait_recv()
 
             @pl.when(group > 0)
@@ -301,6 +316,17 @@
             if not last:
                 halo_start(it + 1, j)
 
+        @pl.loop(0, chunks + 2 + LAG)
+        def _(step):
+            for behind, stage in enumerate((build, convolve, combine)):
+                @pl.when((step >= behind) & (step < chunks + behind))
+                def _(stage=stage, behind=behind):
+                    stage(step - behind)
+
+            @pl.when(step >= 2 + LAG)
+            def _():
+                scan(step - 2 - LAG)
+
     @pl.loop(0, chunks)
     def _(j):
         for it in range(ITERS):
@@ -316,8 +342,7 @@
               w_out, bias_out, drift_coef, eps_coef, noise_coef):
     _, chans, depth, rows, width = trajectory.shape
     hid = w_in.shape[0]
-    chunk = 8 if rows % 8 == 0 else rows
-    block = 4 if rows % 4 == 0 else rows
+    chunk = block = 4 if rows % 4 == 0 else rows
     chunks = rows // chunk
     own, side = depth * chans, 2 * chans
     full, mid = depth + 4, depth + 2
@@ -326,14 +351,21 @@
     flat = chans * depth * rows
     dims = (chans, hid, depth, rows, width, levels, slabs, chunk, block)
     vmem = pl.BlockSpec(memory_space=pltpu.VMEM)
+    hbm = pl.BlockSpec(memory_space=pltpu.HBM)
     smem = pl.BlockSpec(memory_space=pltpu.SMEM)
     dma = pltpu.SemaphoreType.DMA
     result = pl.pallas_call(
         functools.partial(kernel, dims),
         out_shape=jax.ShapeDtypeStruct((flat, width), F32),
-        in_specs=[vmem] * 8 + [smem] * 3,
+        in_specs=[hbm] * 5 + [vmem] * 3 + [smem] * 3,
         out_specs=vmem,
         scratch_shapes=[
+            pltpu.VMEM((flat, width), F32),
+            pltpu.VMEM((flat, width), F32),
+            pltpu.VMEM((flat, width), F32),
+            pltpu.VMEM((27 * chans, hid), BF16),
+            pltpu.VMEM((27 * chans, hid), BF16),
+            dma((5,)),
             pltpu.VMEM((mid * hid, 9 * full * chans), BF16),
             pltpu.VMEM((9 * own, mid * hid), BF16),
             pltpu.VMEM((mid * hid, width), F32),
@@ -360,16 +392,16 @@
             dma((ITERS, chunks)),
         ],
         compiler_params=pltpu.CompilerParams(
-            collective_id=0, has_side_effects=True, vmem_limit_bytes=48 * 1024 * 1024
+            collective_id=0, has_side_effects=True, vmem_limit_bytes=60 * 1024 * 1024
         ),
     )(
         trajectory.reshape(flat, width),
         first_latent.reshape(flat, width),
         noise_draw.reshape(flat, width),
         jnp.transpose(w_in, (2, 3, 4, 1, 0)).reshape(27 * chans, hid),
+        jnp.transpose(w_out, (2, 3, 4, 0, 1)).reshape(27 * chans, hid),
         bias_in[None],
         level_bias,
-        jnp.transpose(w_out, (2, 3, 4, 0, 1)).reshape(27 * chans, hid),
         bias_out[None],
         drift_coef,
         eps_coef,

time: 43.5 us -> 35.2 us (0.81)
  local copies, waits for them, and re-layouts: 5.84 us -> 1.67 us
  Pallas kernels: 35.3 us -> 31.4 us
    unnamed x17 -> x1, local copies, waits for them, and re-layouts: 5.84 us -> 1.67 us
    pallas_call x1, Pallas kernels: 35.3 us -> 31.4 us  [on_device(): pl.pallas_call(functools.partial(kernel, dims), out_shape=jax.ShapeDtypeS...]
where the time goes in v2:
time: 35.2 us; the launch traced here: 35 us
  Pallas kernels  31.4 us (89%)
  between operations  1.95 us (6%)
  local copies, waits for them, and re-layouts  1.67 us (5%)
    pallas_call x1, Pallas kernels, on_device(): pl.pallas_call(functools.partial(kernel, dims), out_shape=jax.ShapeDtypeS...  31.4 us
    unnamed x1, local copies, waits for them, and re-layouts  1.67 us

profile of v2, /device:TPU:24, one launch (start us, length us, event | category | flops | bytes accessed | tf_op | source)
XLA Modules:
  0.0 35.0 jit_solution(2929759872423560498)
XLA Ops:
  1.9 31.4 %shard_map.109 = f32[512,128]{1,0:T(8,128)} custom-call(f32[512,128]{1,0:T(8,128)} %bitcast.13, f32[512,128]{1,0:T(8,128)} %bitcast.14, f32[512,128]{1,0:T(8,128)} %bitcast.15, bf16[216,64]{1,0:T(8,128)(2,1)} %bitcast.16, bf16[216,64]{1,0:T(8,128)(2,1)} %bitcast.17, f32[1,64]{1,0:T(1,128)} %bitcast.18, f32[1,64]{1,0:T(1,128)} %level_bias.1, ...), custom_call_target="tpu_custom_call" | custom-call | tf_op jit(solution)/shard_map/pallas_call | solution.py:357
  33.3 1.7 %copy.16 = f32[1,8,2,32,128]{4,3,2,1,0:T(8,128)} copy(f32[1,8,2,32,128]{4,3,2,1,0:T(8,128)} %bitcast.12) | data formatting | bytes 524288
